TPU v7x, 32 devices: a whole 2x2x4 slice. The times are simulated.
32 devices in a mesh: lat: 4 (over x, core), lev: 8 (over z, y).
Axes of the slice: x: 2, y: 2, z: 4, core: 2. Of those that a mesh axis runs over, the one named last changes fastest.
Arguments:
- fields: bfloat16 [6, 16, 32, 1152], P(None, 'lev', 'lat'), may hold values from -6 to 6
- courant: bfloat16 [16, 32, 1152], P('lev', 'lat'), may hold values from -0.8984375 to 0.8984375
- filter_matrix: bfloat16 [1152, 1152], replicated, may hold values from -0.1875 to 0.1875
- polar_mask: int32 [32], P('lat'), may hold values from 0 to 1, as said below
- band_start: int32 [16], replicated, may hold values from 0 to 12, as said below
- remap_weights: float32 [32, 16, 4], P('lat'), may hold values from 0.05 to 0.5
Outputs:
- remapped: bfloat16 [6, 16, 32, 1152], P(None, 'lev', 'lat')
Inputs may be any that keep to these rules, and one draw needn't show every extreme that they name: `polar_mask`: 1 on a run of 4 to 8 latitudes at each pole, 0 elsewhere. band_start[0] is 0 and band_start[15] is 12.
All inputs are finite; a program needn't handle non-finite values.
Results may differ from a plain program's by a relative error of at most 0.0052.
Values may be sent and summed in bfloat16 or wider, within the bound.
No kernel may reach another device: no remote copies, remote signals or barrier semaphores. Data moves between devices by JAX's collectives and lax.ppermute only.
A program may use at most 64 MiB of HBM per device.

v0:
```python
import jax
import jax.numpy as jnp
from jax import lax
from jax.sharding import PartitionSpec as P


def padded_2(block, sides, width):
    for axis, dim in sides:
        count = lax.axis_size(axis)
        forward = [(i, i + 1) for i in range(count - 1)]
        backward = [(target, source) for source, target in forward]
        low = lax.ppermute(
            lax.slice_in_dim(block, block.shape[dim] - width, None, axis=dim), axis, forward
        )
        high = lax.ppermute(lax.slice_in_dim(block, 0, width, axis=dim), axis, backward)
        block = jnp.concatenate([low, block, high], axis=dim)
    return block


def on_device(fields, courant, filter_matrix, polar_mask, band_start, remap_weights):
    field_count = fields.shape[0]
    level_rows = fields.shape[1]
    lat_rows = fields.shape[2]
    lon_total = fields.shape[3]
    band_width = remap_weights.shape[2]
    level_total = band_start.shape[0]
    lat_total = lat_rows * lax.axis_size("lat")
    first_row = lax.axis_index("lat") * lat_rows
    stacked = jnp.concatenate([fields, courant[None]], axis=0)
    extended = padded_2(stacked, (("lat", 2),), 2)
    padded = extended[:field_count].astype(jnp.float32)
    speed_pad = extended[field_count].astype(jnp.float32)
    face_index = first_row + jnp.arange(lat_rows + 1, dtype=jnp.int32) - 1
    face_live = ((face_index >= 0) & (face_index <= lat_total - 2)).astype(jnp.float32)[
        None, :, None
    ]
    face_speed = 0.5 * (speed_pad[:, 1 : lat_rows + 2] + speed_pad[:, 2 : lat_rows + 3]) * face_live
    face_flux = (
        face_speed[None]
        * (
            7.0 * (padded[:, :, 1 : lat_rows + 2] + padded[:, :, 2 : lat_rows + 3])
            - (padded[:, :, 0 : lat_rows + 1] + padded[:, :, 3 : lat_rows + 4])
        )
        / 12.0
    )
    moved_field = padded[:, :, 2 : lat_rows + 2] - (face_flux[:, :, 1:] - face_flux[:, :, :-1])
    moved_low = moved_field.astype(jnp.bfloat16)
    correction = jnp.dot(
        moved_low.reshape(-1, lon_total), filter_matrix, preferred_element_type=jnp.float32
    ).reshape(moved_field.shape)
    polar_rows = (polar_mask == 1)[None, None, :, None]
    filtered = (moved_field + jnp.where(polar_rows, correction, 0.0)).astype(jnp.bfloat16)
    flat_cells = lat_rows * lon_total
    flat_filtered = filtered.reshape(field_count, level_rows, flat_cells)
    piece_cells = flat_cells // lax.axis_size("lev")
    cell_index = lax.axis_index("lev") * piece_cells + jnp.arange(piece_cells, dtype=jnp.int32)
    cell_lat = cell_index // lon_total
    lat_onehot = (jnp.arange(lat_rows, dtype=jnp.int32)[:, None] == cell_lat[None, :]).astype(
        jnp.float32
    )
    band_weights = jnp.transpose(remap_weights, (2, 1, 0))
    cell_weights = jnp.einsum(
        "btl,lp->btp", band_weights, lat_onehot, precision=lax.Precision.HIGHEST
    )
    source_index = jnp.arange(level_total, dtype=jnp.int32)[None, None, :]
    band_offset = jnp.arange(band_width, dtype=jnp.int32)[:, None, None]
    selection = (source_index == band_start[None, :, None] + band_offset).astype(jnp.bfloat16)
    columns = lax.all_to_all(flat_filtered, "lev", split_axis=2, concat_axis=1, tiled=True)
    total = jnp.zeros(columns.shape, jnp.float32)
    for offset in range(band_width):
        source = jnp.einsum(
            "ts,fsp->ftp", selection[offset], columns, preferred_element_type=jnp.float32
        )
        total = total + cell_weights[offset][None] * source
    flat_out = lax.all_to_all(
        total.astype(jnp.bfloat16), "lev", split_axis=1, concat_axis=2, tiled=True
    )
    return flat_out.reshape(field_count, level_rows, lat_rows, lon_total)


def solution(mesh):
    return jax.shard_map(
        on_device,
        mesh=mesh,
        in_specs=(
            P(None, "lev", "lat", None),
            P("lev", "lat", None),
            P(),
            P("lat"),
            P(),
            P("lat", None, None),
        ),
        out_specs=P(None, "lev", "lat", None),
        check_vma=False,
    )
```

profile of v0, /device:TPU:0, one launch (start us, length us, event | category | flops | bytes accessed | tf_op | source)
XLA Modules:
  0.0 78.7 jit_solution(10582550394847013708)
XLA Ops:
  0.0 0.0 copy-start
  0.0 0.0 copy-start.2
  0.0 0.0 copy-start.1
  0.0 1.3 %pad_maximum_fusion.2 = (bf16[7,2,2,1152]{3,2,1,0:T(2,128)(2,1)S(1)}, bf16[7,2,2,1152]{3,2,1,0:T(2,128)(2,1)S(1)}) fusion(bf16[1,2,8,1152]{3,2,1,0:T(8,128)(2,1)} %bitcast.88, bf16[6,2,8,1152]{3,2,1,0:T(8,128)(2,1)} %param.6), kind=kLoop, calls=%fused_computation.39 | loop fusion | flops 258048 | bytes 387072 | tf_op jit(solution)/shard_map/slice | solution.py:13
  1.3 2.4 %collective-permute-start = (bf16[7,2,2,1152]{3,2,1,0:T(2,128)(2,1)S(1)}, bf16[7,2,2,1152]{3,2,1,0:T(2,128)(2,1)S(1)}, u32[]{:S(2)}, u32[]{:S(2)}) collective-permute-start(bf16[7,2,2,1152]{3,2,1,0:T(2,128)(2,1)S(1)} %get-tuple-element.9), channel_id=1, source_target_pairs={{0,8},{8,16},{16,24},{1,9},{9,17},{17,25},{2,10},{10,18},{18,26},{... | collective-permute-start | bytes 193544 | tf_op jit(solution)/shard_map/ppermute | solution.py:12
  3.7 1.3 %collective-permute-start.1 = (bf16[7,2,2,1152]{3,2,1,0:T(2,128)(2,1)S(1)}, bf16[7,2,2,1152]{3,2,1,0:T(2,128)(2,1)S(1)}, u32[]{:S(2)}, u32[]{:S(2)}) collective-permute-start(bf16[7,2,2,1152]{3,2,1,0:T(2,128)(2,1)S(1)} %get-tuple-element.10), channel_id=1, source_target_pairs={{8,0},{16,8},{24,16},{9,1},{17,9},{25,17},{10,2},{18,10},{26,18},{... | collective-permute-start | bytes 193544 | tf_op jit(solution)/shard_map/ppermute | solution.py:15
  5.0 0.7 broadcast_compare_fusion
  5.7 0.7 iota_add_fusion.1
  6.4 0.1 iota_compare_fusion.1
  6.4 1.0 %convolution_bitcast_fusion.4 = f32[4,16,1152]{2,1,0:T(8,128)S(1)} fusion(s32[1152]{0:T(1024)S(1)} %add_select_fusion, f32[4,16,8]{1,0,2:T(4,128)} %bitcast.91), kind=kOutput, calls=%fused_computation.17 | convolution fusion | flops 7087104 | bytes 301568 | tf_op jit(solution)/shard_map/btl,lp->btp/dot_general | solution.py:62
  7.5 0.0 collective-permute-done
  7.5 1.4 %collective-permute-done.1 = bf16[7,2,2,1152]{3,2,1,0:T(2,128)(2,1)S(1)} collective-permute-done((bf16[7,2,2,1152]{3,2,1,0:T(2,128)(2,1)S(1)}, bf16[7,2,2,1152]{3,2,1,0:T(2,128)(2,1)S(1)}, u32[]{:S(2)}, u32[]{:S(2)}) %collective-permute-start.1) | collective-permute-done | bytes 64544 | tf_op jit(solution)/shard_map/ppermute | solution.py:15
  9.0 1.2 %pad_maximum_fusion = bf16[7,2,12,1152]{3,2,1,0:T(8,128)(2,1)S(1)} fusion(bf16[7,2,2,1152]{3,2,1,0:T(2,128)(2,1)S(1)} %collective-permute-done.1, bf16[1,2,8,1152]{3,2,1,0:T(8,128)(2,1)} %bitcast.89, bf16[6,2,8,1152]{3,2,1,0:T(8,128)(2,1)} %param.6, bf16[7,2,2,1152]{3,2,1,0:T(2,128)(2,1)S(1)} %collective-permute-done), kind=kLoop, calls=%fused_computation.24 | loop fusion | flops 1548288 | bytes 774144 | tf_op jit(solution)/shard_map/concatenate | solution.py:16
  10.2 0.1 slice_convert_fusion
  10.3 0.0 copy-done.2
  10.3 0.0 copy-done.1
  10.3 0.1 fusion.26
  10.4 0.3 fusion.21
  10.8 0.0 copy-done
  10.8 0.7 fusion.16
  11.4 5.7 %copy.21 = bf16[6,2,8,1152]{0,1,3,2:T(2,128)(2,1)} copy(bf16[6,2,8,1152]{3,2,1,0:T(8,128)(2,1)S(1)} %fusion.16) | data formatting | bytes 442368 | tf_op jit(solution)/shard_map/reshape | solution.py:54
  17.2 9.0 %reshape.64 = bf16[8,2,6912]{2,1,0:T(2,128)(2,1)} reshape(bf16[9216,2,6]{2,1,0:T(2,128)(2,1)} %bitcast.84) | data formatting | bytes 442368
  26.1 5.8 %all-to-all-start = ((bf16[8,2,6912]{2,1,0:T(2,128)(2,1)}), bf16[8,2,6912]{2,1,0:T(2,128)(2,1)S(1)}, u32[]{:S(2)}, u32[]{:S(2)}) async-start(bf16[8,2,6912]{2,1,0:T(2,128)(2,1)} %reshape.64), calls=%async_computation | async-start | bytes 442368 | tf_op jit(solution)/shard_map/all_to_all | solution.py:68
  32.0 8.0 %all-to-all-done = bf16[8,2,6912]{2,1,0:T(2,128)(2,1)S(1)} async-done(((bf16[8,2,6912]{2,1,0:T(2,128)(2,1)}), bf16[8,2,6912]{2,1,0:T(2,128)(2,1)S(1)}, u32[]{:S(2)}, u32[]{:S(2)}) %all-to-all-start) | async-done | bytes 221216 | tf_op jit(solution)/shard_map/all_to_all | solution.py:68
  40.0 11.8 %reshape.65 = bf16[9216,2,6]{2,1,0:T(2,128)(2,1)} reshape(bf16[8,2,6912]{2,1,0:T(2,128)(2,1)S(1)} %all-to-all-done) | data formatting | bytes 442368
  51.8 10.1 %copy.17 = bf16[6,2,8,1152]{3,1,2,0:T(2,128)(2,1)S(1)} copy(bf16[6,2,8,1152]{0,1,3,2:T(2,128)(2,1)} %bitcast.85) | data formatting | bytes 442368 | tf_op jit(solution)/shard_map/all_to_all | solution.py:68
  61.9 0.1 all_to_all.27
  62.0 0.2 fusion.14
  62.2 0.2 fusion.13
  62.4 0.2 fusion.11
  62.6 0.2 fusion.15
  62.8 0.1 copy.18
  62.8 15.2 %all_to_all.33 = bf16[6,16,1152]{2,0,1:T(8,128)(2,1)S(1)} all-to-all(bf16[6,16,1152]{2,0,1:T(8,128)(2,1)S(1)} %copy.18), channel_id=1, replica_groups=mesh['lat'=4,'lev'=8] {'lev'}, dimensions={1} | all-to-all | bytes 442368 | tf_op jit(solution)/shard_map/all_to_all | solution.py:75
  78.0 0.7 copy.25
  (4 shorter events, 0.1 us)
Async XLA Ops:
  0.0 10.8 %copy-start = (bf16[1152,1152]{1,0:T(8,128)(2,1)S(1)}, bf16[1152,1152]{1,0:T(8,128)(2,1)}, u32[]{:S(2)}) copy-start(bf16[1152,1152]{1,0:T(8,128)(2,1)} %param.8) | copy-start | bytes 7962628
  0.0 10.3 %copy-start.2 = (bf16[2,8,1152]{2,1,0:T(8,128)(2,1)S(1)}, bf16[2,8,1152]{2,1,0:T(8,128)(2,1)}, u32[]{:S(2)}) copy-start(bf16[2,8,1152]{2,1,0:T(8,128)(2,1)} %param.7) | copy-start | bytes 110596
  0.0 10.3 %copy-start.1 = (bf16[6,2,8,1152]{3,2,1,0:T(8,128)(2,1)S(1)}, bf16[6,2,8,1152]{3,2,1,0:T(8,128)(2,1)}, u32[]{:S(2)}) copy-start(bf16[6,2,8,1152]{3,2,1,0:T(8,128)(2,1)} %param.6) | copy-start | bytes 663556
  1.3 6.2 %collective-permute-start = (bf16[7,2,2,1152]{3,2,1,0:T(2,128)(2,1)S(1)}, bf16[7,2,2,1152]{3,2,1,0:T(2,128)(2,1)S(1)}, u32[]{:S(2)}, u32[]{:S(2)}) collective-permute-start(bf16[7,2,2,1152]{3,2,1,0:T(2,128)(2,1)S(1)} %get-tuple-element.9), channel_id=1, source_target_pairs={{0,8},{8,16},{16,24},{1,9},{9,17},{17,25},{2,10},{10,18},{18,26},{... | collective-permute-start | bytes 193544 | tf_op jit(solution)/shard_map/ppermute | solution.py:12
  3.7 5.3 %collective-permute-start.1 = (bf16[7,2,2,1152]{3,2,1,0:T(2,128)(2,1)S(1)}, bf16[7,2,2,1152]{3,2,1,0:T(2,128)(2,1)S(1)}, u32[]{:S(2)}, u32[]{:S(2)}) collective-permute-start(bf16[7,2,2,1152]{3,2,1,0:T(2,128)(2,1)S(1)} %get-tuple-element.10), channel_id=1, source_target_pairs={{8,0},{16,8},{24,16},{9,1},{17,9},{25,17},{10,2},{18,10},{26,18},{... | collective-permute-start | bytes 193544 | tf_op jit(solution)/shard_map/ppermute | solution.py:15
  26.1 13.8 %all-to-all-start = ((bf16[8,2,6912]{2,1,0:T(2,128)(2,1)}), bf16[8,2,6912]{2,1,0:T(2,128)(2,1)S(1)}, u32[]{:S(2)}, u32[]{:S(2)}) async-start(bf16[8,2,6912]{2,1,0:T(2,128)(2,1)} %reshape.64), calls=%async_computation | async-start | bytes 442368 | tf_op jit(solution)/shard_map/all_to_all | solution.py:68
where the time goes:
time: 79.3 us; the launch traced here: 78.7 us
  local copies, waits for them, and re-layouts  37.5 us (47%)
  blocking collectives  15.2 us (19%)
  starting transfers between devices  9.5 us (12%)
  waiting for transfers between devices  9.4 us (12%)
  other arithmetic  4.5 us (6%)
  matrix products  2.48 us (3%)
    unnamed x8, local copies, waits for them, and re-layouts  20.8 us
    all_to_all x1, blocking collectives, on_device(): lax.all_to_all(total.astype(jnp.bfloat16), 'lev', split_axis=1, concat_ax...  15.2 us
    all_to_all x2, local copies, waits for them, and re-layouts, on_device(): lax.all_to_all(flat_filtered, 'lev', split_axis=2, concat_axis=1, tiled=T...  10.2 us
    all_to_all x1, waiting for transfers between devices, on_device(): lax.all_to_all(flat_filtered, 'lev', split_axis=2, concat_axis=1, tiled=T...  7.95 us
    all_to_all x1, starting transfers between devices, on_device(): lax.all_to_all(flat_filtered, 'lev', split_axis=2, concat_axis=1, tiled=T...  5.84 us
    reshape x1, local copies, waits for them, and re-layouts, on_device(): flat_filtered = filtered.reshape(field_count, level_rows, flat_cells)  5.73 us
    ppermute x1, starting transfers between devices, padded_2(): lax.ppermute(lax.slice_in_dim(block, block.shape[dim] - width, None, axis...  2.37 us
  transfers between devices with their start and end apart: 3, of which 2 were waited for; matrix products, arithmetic and copies ran while one was open for 3% of the time, Pallas kernels for 0%

commit v1 on v0

v1 whole, which is shorter than its diff:
```python
import functools

import jax
import jax.numpy as jnp
from jax import lax
from jax.experimental import pallas as pl
from jax.experimental.pallas import tpu as pltpu
from jax.sharding import PartitionSpec as P

WIDTH = 2
LANES = 128
EDGE_ROWS = 32
PARTS = 2
VMEM_LIMIT = 48 * 1024 * 1024
WHOLE = pl.BlockSpec(memory_space=pltpu.VMEM)


def cost(flops, moved):
    return pl.CostEstimate(flops=flops, bytes_accessed=moved, transcendentals=0)


def params():
    return pltpu.CompilerParams(vmem_limit_bytes=VMEM_LIMIT)


def exchange_order(count):
    order = list(range(count - 2, -1, -2)) + list(range(1, count, 2))
    return order[-3:] + order[:-3]


def member_at(position, count):
    member = jnp.zeros_like(position)
    for place, index in enumerate(exchange_order(count)):
        member = jnp.where(position == place, index, member)
    return member


def in_hbm(array):
    return pltpu.with_memory_space_constraint(array, pltpu.HBM)


def in_vmem(array):
    return pltpu.with_memory_space_constraint(array, pltpu.VMEM)


def iota(shape, axis):
    return lax.broadcasted_iota(jnp.int32, shape, axis)


def edge_shape(field_edges, levels, lon):
    pieces = max(p for p in range(1, 8 // levels + 1) if lon // LANES % p == 0)
    return 8, field_edges // 8 * lon + lon // pieces


def write_edges(ref, edges, field_edges, levels):
    lon = edges.shape[1]
    groups = field_edges // 8
    for group in range(groups):
        part = edges[group * 8 : group * 8 + 8]
        ref[:, group * lon : (group + 1) * lon] = part.astype(jnp.bfloat16)
    width = ref.shape[1] - groups * lon
    courant = edges[field_edges : field_edges + levels]
    parts = [courant[:, at : at + width] for at in range(0, lon, width)]
    rest = 8 - len(parts) * levels
    if rest:
        parts.append(jnp.zeros((rest, width), jnp.float32))
    ref[:, groups * lon :] = jnp.concatenate(parts, axis=0).astype(jnp.bfloat16)


def read_edges(ref, field_edges, levels, lon):
    groups = field_edges // 8
    edges = ref[...].astype(jnp.float32)
    fields = [edges[:, group * lon : (group + 1) * lon] for group in range(groups)]
    width = edges.shape[1] - groups * lon
    courant = [
        edges[part * levels : (part + 1) * levels, groups * lon :] for part in range(lon // width)
    ]
    return fields, jnp.concatenate(courant, axis=1)


def write_stencil(stencil_ref, field_count, levels, rows):
    count = field_count * levels * rows
    speed_count = levels * rows
    lat = lax.axis_index("lat")
    lats = lax.axis_size("lat")
    odd = lat % 2

    own = (field_count + 1) * speed_count
    field_edges = field_count * levels * WIDTH
    column = iota((1, stencil_ref.shape[1]), 1)
    edge = column - own
    speed_edge = edge - 2 * field_edges
    is_own, is_speed = edge < 0, speed_edge >= 0
    far = jnp.where(is_speed, speed_edge // levels, edge // field_edges)
    field_edge = edge - far * field_edges
    edge_block = jnp.where(
        is_speed, speed_edge - far * levels + field_count * levels, field_edge // WIDTH
    )
    sides = jnp.where((lat > 0) & (lat < lats - 1), 2, 1)
    block = jnp.where(is_own, column // rows, jnp.where(far < sides, edge_block, -1))
    high = (odd + far + 1) % 2
    edge_place = jnp.where(is_speed, high * (rows + 1) - 1, field_edge % WIDTH - WIDTH + high * (rows + WIDTH))
    place = jnp.where(is_own, column % rows, edge_place)

    def relation(height, first_block):
        line = iota((height, 1), 0)
        line_block = line // rows
        row = line - line_block * rows
        return row, place - row, block == line_block + first_block

    def near_face(here, shift):
        return (here == shift) | (here == shift - 1)

    _, here, same = relation(count, 0)
    for side in range(2):
        outer = (here == side + 1) | (here == side - 2)
        value = jnp.where(near_face(here, side), 7.0, jnp.where(outer, -1.0, 0.0))
        stencil_ref[side * count : (side + 1) * count] = jnp.where(same, value, 0.0).astype(
            jnp.bfloat16
        )
    row, here, same = relation(speed_count, field_count * levels)
    live = ((row > 0) | (lat > 0), (row < rows - 1) | (lat < lats - 1))
    for side in range(2):
        first = 2 * count + side * speed_count
        value = jnp.where(same & near_face(here, side) & live[side], 0.5, 0.0)
        stencil_ref[first : first + speed_count] = value.astype(jnp.bfloat16)


def write_band_matrix(band_matrix_ref, polar_ref, mask_ref, band_ref, weight_ref, rows, levels):
    polar_row = iota(polar_ref.shape, 0)
    polar = jnp.zeros(polar_ref.shape, jnp.int32)
    for index in range(rows):
        polar = jnp.where(polar_row == index, mask_ref[:, index : index + 1], polar)
    polar_ref[...] = polar

    band_width, level_total = weight_ref.shape[1:]
    total = level_total * rows

    def level_at(index):
        place = index // rows
        position = place // levels
        return (member_at(position, level_total // levels) - position) * levels + place

    out_row, in_row = iota((total, 1), 0), iota((1, total), 1)
    of_row = level_at(out_row) == iota((1, level_total), 1)

    def spread(table):
        whole = jnp.concatenate([table] * level_total, axis=0)
        return jnp.sum(jnp.where(of_row, whole, jnp.zeros_like(whole)), axis=1, keepdims=True)

    start = spread(jnp.broadcast_to(band_ref[...], (rows, level_total)))
    offset = level_at(in_row) - start
    matrix = jnp.zeros((total, total), jnp.float32)
    for band in range(band_width):
        matrix = jnp.where(offset == band, spread(weight_ref[:, band, :]), matrix)
    matrix = jnp.where(in_row % rows == out_row % rows, matrix, 0.0)
    for part in range(PARTS):
        rounded = matrix.astype(jnp.bfloat16)
        band_matrix_ref[part * total : (part + 1) * total] = rounded
        matrix = matrix - rounded.astype(jnp.float32)


def edges_body(
    filter_hbm, fields_hbm, courant_hbm, mask_hbm, band_hbm, weight_hbm,
    near_ref, far_ref, stack_ref, stencil_ref, polar_ref, band_matrix_ref,
    mask_ref, band_ref, weight_ref, sems,
    *, field_count, levels, rows
):
    own = stack_ref.shape[0]
    blocks = own // rows
    field_rows = field_count * levels * rows
    pairs = (
        (fields_hbm, stack_ref.at[pl.ds(0, field_rows)]),
        (courant_hbm, stack_ref.at[pl.ds(field_rows, own - field_rows)]),
        (weight_hbm, weight_ref),
        (band_hbm, band_ref),
        (mask_hbm, mask_ref),
    )
    copies = [
        pltpu.make_async_copy(source, target, sems.at[index])
        for index, (source, target) in enumerate(pairs)
    ]
    for copy in copies:
        copy.start()
    odd = lax.axis_index("lat") % 2
    edge = iota((2 * EDGE_ROWS, 1), 0)
    far = (edge >= EDGE_ROWS).astype(jnp.int32)
    inner = edge - far * EDGE_ROWS
    high = (odd + far + 1) % 2
    field_edges = field_count * levels * WIDTH
    of_field = inner < field_edges
    block = jnp.where(of_field, inner // WIDTH, inner - field_edges + field_count * levels)
    row = jnp.where(of_field, inner % WIDTH + high * (rows - WIDTH), high * (rows - 1))
    wanted = jnp.where(block < blocks, block * rows + row, -1)
    pick = jnp.where(iota((2 * EDGE_ROWS, own), 1) == wanted, 1.0, 0.0).astype(jnp.bfloat16)
    write_stencil(stencil_ref, field_count, levels, rows)
    for copy in copies[2:]:
        copy.wait()
    write_band_matrix(band_matrix_ref, polar_ref, mask_ref, band_ref, weight_ref, rows, levels)
    for copy in copies[:2]:
        copy.wait()
    edges = jnp.dot(pick, stack_ref[...], preferred_element_type=jnp.float32)
    write_edges(near_ref, edges[:EDGE_ROWS], field_edges, levels)
    for member in range(2):
        write_edges(far_ref.at[member], edges[EDGE_ROWS:], field_edges, levels)


def tiles(field_count, levels, lon, units):
    for field in range(field_count):
        for part in range(lon // LANES):
            unit = field * (lon // LANES) + part
            for level in range(levels):
                yield field, level, part * LANES, (unit // units, unit % units, level)


def transport_body(
    near_ref, far_ref, stack_ref, stencil_ref, filter_ref, polar_ref, out_ref, *, field_count
):
    pieces, units, levels, rows, _ = out_ref.shape
    lon = stack_ref.shape[1]
    count = field_count * levels * rows
    speed_count = levels * rows
    field_edges = field_count * levels * WIDTH
    near_fields, near_courant = read_edges(near_ref, field_edges, levels, lon)
    partner = lax.axis_index("lat") % 2
    far_fields, far_courant = read_edges(far_ref.at[partner], field_edges, levels, lon)
    rest = EDGE_ROWS // 2 - 2 * levels
    speeds = [near_courant, far_courant, jnp.zeros((rest, lon), jnp.float32)]
    edges = jnp.concatenate(
        near_fields + far_fields + [jnp.concatenate(speeds, axis=0)], axis=0
    )
    source = jnp.concatenate([stack_ref[...], edges.astype(jnp.bfloat16)], axis=0)
    values = jnp.dot(stencil_ref[...], source, preferred_element_type=jnp.float32)
    speed_low = values[2 * count : 2 * count + speed_count] * (1.0 / 12.0)
    speed_high = values[2 * count + speed_count :] * (1.0 / 12.0)
    parts = []
    for first in range(0, count, speed_count):
        flux_low = speed_low * values[first : first + speed_count]
        flux_high = speed_high * values[count + first : count + first + speed_count]
        own = stack_ref[first : first + speed_count].astype(jnp.float32)
        parts.append(own - (flux_high - flux_low))
    moved = jnp.concatenate(parts, axis=0)

    def write(filtered):
        for field, level, at, place in tiles(field_count, levels, lon, units):
            first = (field * levels + level) * rows
            tile = filtered[first : first + rows, at : at + LANES]
            out_ref[place] = tile.astype(jnp.bfloat16)
        for unit in range(field_count * lon // LANES, pieces * units):
            out_ref[unit // units, unit % units] = jnp.zeros(out_ref.shape[2:], jnp.bfloat16)

    polar = polar_ref[...] == 1
    any_polar = jnp.max(polar_ref[...]) == 1

    @pl.when(any_polar)
    def _():
        correction = jnp.dot(
            moved.astype(jnp.bfloat16), filter_ref[...], preferred_element_type=jnp.float32
        )
        wide = jnp.concatenate([polar] * (lon // LANES), axis=1)
        whole = jnp.concatenate([wide] * (field_count * levels), axis=0)
        write(moved + jnp.where(whole, correction, 0.0))

    @pl.when(jnp.logical_not(any_polar))
    def _():
        write(moved)


def remap_body(band_matrix_ref, source_ref, out_ref):
    pieces, units, levels, rows, _ = source_ref.shape
    total = pieces * levels * rows
    columns = jnp.concatenate(
        [
            source_ref[:, unit].astype(jnp.float32).reshape(total, LANES).astype(jnp.bfloat16)
            for unit in range(units)
        ],
        axis=1,
    )
    split = jnp.dot(band_matrix_ref[...], columns, preferred_element_type=jnp.float32)
    result = split[(PARTS - 1) * total :]
    for part in range(PARTS - 1)[::-1]:
        result = result + split[part * total : (part + 1) * total]
    for unit in range(units):
        part = result[:, unit * LANES : (unit + 1) * LANES]
        out_ref[:, unit] = part.reshape(pieces, levels, rows, LANES).astype(jnp.bfloat16)


def collect_body(source_ref, out_hbm, out_ref, sems):
    field_count, levels, _, lon = out_ref.shape
    units = source_ref.shape[1]
    copies = []
    for field, level, at, place in tiles(field_count, levels, lon, units):
        out_ref[field, level, :, at : at + LANES] = source_ref[place]
        if at + LANES == lon and level == levels - 1:
            copy = pltpu.make_async_copy(out_ref.at[field], out_hbm.at[field], sems.at[field])
            copy.start()
            copies.append(copy)
    for copy in copies:
        copy.wait()


def on_device(fields, courant, filter_matrix, polar_mask, band_start, remap_weights):
    def array(*shape, dtype=jnp.bfloat16):
        return jax.ShapeDtypeStruct(shape, dtype)

    field_count, levels, rows, lon = fields.shape
    lats, levs = lax.axis_size("lat"), lax.axis_size("lev")
    level_total, band_width = remap_weights.shape[1:]
    if lon % LANES or rows % 8:
        raise ValueError("uneven tiles")
    units = -(-(field_count * lon // LANES) // levs)
    count = field_count * levels * rows
    blocks = (field_count + 1) * levels
    own = blocks * rows
    field_edges = field_count * levels * WIDTH
    if field_edges % 8 or 8 % levels or field_edges + levels > EDGE_ROWS:
        raise ValueError("uneven edges")
    edges = array(*edge_shape(field_edges, levels, lon))
    total = level_total * rows

    hbm = pl.BlockSpec(memory_space=pltpu.HBM)
    sizes = dict(field_count=field_count, levels=levels, rows=rows)
    small = [
        polar_mask.reshape(1, -1),
        band_start.reshape(1, -1),
        jnp.swapaxes(remap_weights, 1, 2),
    ]
    inputs = [filter_matrix, fields.reshape(count, lon), courant.reshape(own - count, lon), *small]
    near, far, stack, stencil, polar, band_matrix = pl.pallas_call(
        functools.partial(edges_body, **sizes),
        out_shape=(
            edges,
            array(2, *edges.shape),
            array(own, lon),
            array(2 * (count + levels * rows), own + 2 * field_edges + EDGE_ROWS // 2),
            array(rows, LANES, dtype=jnp.int32),
            array(PARTS * total, total),
        ),
        in_specs=[hbm] * len(inputs),
        out_specs=(WHOLE,) * 6,
        scratch_shapes=[pltpu.VMEM(each.shape, each.dtype) for each in small]
        + [pltpu.SemaphoreType.DMA((len(inputs) - 1,))],
        compiler_params=params(),
        cost_estimate=cost(2 * own * own * lon, 4 * own * lon),
    )(*map(in_hbm, inputs))

    near_pairs = [(i, i + 1) for i in range(0, lats - 1, 2)]
    from_near = lax.ppermute(
        near, "lat", near_pairs + [(target, source) for source, target in near_pairs]
    )
    far_groups = [[i, i + 1] for i in range(1, lats - 1, 2)] + [[0, lats - 1]]

    def exchange_far(array):
        return lax.all_to_all(
            array, "lat", split_axis=0, concat_axis=0, tiled=True, axis_index_groups=far_groups
        )

    lat_index = lax.axis_index("lat")
    has_far = (lat_index > 0) & (lat_index < lats - 1)
    from_far = lax.cond(has_far, exchange_far, lambda array: array, far)

    pieces = pl.pallas_call(
        functools.partial(transport_body, field_count=field_count),
        out_shape=array(levs, units, levels, rows, LANES),
        in_specs=[WHOLE] * 6,
        out_specs=WHOLE,
        compiler_params=params(),
        cost_estimate=cost(2 * count * lon * lon, 2 * lon * lon),
    )(from_near, from_far, stack, stencil, in_vmem(filter_matrix), polar)

    def exchange(array):
        group = exchange_order(levs)
        return lax.all_to_all(
            array, "lev", split_axis=0, concat_axis=0, tiled=True, axis_index_groups=[group]
        )

    remapped = pl.pallas_call(
        remap_body,
        out_shape=array(*pieces.shape),
        in_specs=[WHOLE] * 2,
        out_specs=WHOLE,
        compiler_params=params(),
        cost_estimate=cost(6 * total * total * units * LANES, 4 * total * units * LANES),
    )(band_matrix, exchange(pieces))
    return pl.pallas_call(
        collect_body,
        out_shape=array(*fields.shape),
        in_specs=[WHOLE],
        out_specs=hbm,
        scratch_shapes=[
            pltpu.VMEM(fields.shape, fields.dtype),
            pltpu.SemaphoreType.DMA((field_count,)),
        ],
        compiler_params=params(),
        cost_estimate=cost(count * lon, 4 * count * lon),
    )(exchange(remapped))


def solution(mesh):
    return jax.shard_map(
        on_device,
        mesh=mesh,
        in_specs=(
            P(None, "lev", "lat", None),
            P("lev", "lat", None),
            P(),
            P("lat"),
            P(),
            P("lat", None, None),
        ),
        out_specs=P(None, "lev", "lat", None),
        check_vma=False,
    )
```

time: 79.3 us -> 30.3 us (0.38)
  the two profiles are of different devices: /device:TPU:0 before, /device:TPU:1 now
where the time goes in v1:
time: 30.3 us; the launch traced here: 29.9 us
  blocking collectives  26.9 us (89%)
  Pallas kernels  2.79 us (9%)
    all_to_all x2, blocking collectives, exchange(): lax.all_to_all(array, 'lev', split_axis=0, concat_axis=0, tiled=True, axi...  19.4 us
    all_to_all x1, blocking collectives, exchange_far(): lax.all_to_all(array, 'lat', split_axis=0, concat_axis=0, tiled=True, axi...  7.51 us
    pallas_call x1, Pallas kernels, on_device(): pl.pallas_call(functools.partial(edges_body, **sizes), out_shape=(edges,...  1.43 us
    pallas_call x1, Pallas kernels, on_device(): pl.pallas_call(collect_body, out_shape=array(*fields.shape), in_specs=[WH...  0.74 us
  transfers between devices with their start and end apart: 1, of which 0 were waited for; matrix products, arithmetic and copies ran while one was open for 0% of the time, Pallas kernels for 0%

profile of v1, /device:TPU:1, one launch (start us, length us, event | category | flops | bytes accessed | tf_op | source)
XLA Modules:
  0.0 29.9 jit_solution(3159901165087284078)
XLA Ops:
  0.0 0.0 copy-start
  0.0 1.4 %shard_map.64 = (bf16[8,3840]{1,0:T(8,128)(2,1)S(1)}, bf16[2,8,3840]{2,1,0:T(8,128)(2,1)S(1)}, bf16[112,1152]{1,0:T(8,128)(2,1)S(1)}, bf16[224,176]{1,0:T(8,128)...) custom-call(bf16[1152,1152]{1,0:T(8,128)(2,1)} %filter_ref.1, bf16[96,1152]{1,0:T(8,128)(2,1)} %bitcast.5, ...), custom_call_target="tpu_custom_call" | custom-call | flops 28901376 | bytes 516096 | tf_op jit(solution)/shard_map/pallas_call | solution.py:329
  1.4 0.1 collective-permute-start
  1.6 7.5 %conditional.1 = (bf16[2,8,3840]{2,1,0:T(8,128)(2,1)S(1)}) conditional(s32[]{:T(128)} %convert_element_type.3, bf16[2,8,3840]{2,1,0:T(8,128)(2,1)S(1)} %get-tuple-element.18, bf16[2,8,3840]{2,1,0:T(8,128)(2,1)S(1)} %get-tuple-element.18), branch_computations={%region_0.0_spmd, %region_1.0_spmd} | conditional | bytes 491528 | solution.py:360
  1.6 7.5 %all_to_all.14 = bf16[2,8,3840]{2,1,0:T(8,128)(2,1)S(1)} all-to-all(bf16[2,8,3840]{2,1,0:T(8,128)(2,1)S(1)} %copy.9), channel_id=1, replica_groups={{8,16},{0,24},{9,17},{1,25},{10,18},{2,26},{11,19},{3,27},{12,20},{4,28..., dimensions={0} | all-to-all | bytes 245760 | tf_op jit(solution)/shard_map/cond/branch_1_fun/all_to_all | solution.py:354
  9.1 0.0 collective-permute-done.near_ref
  9.1 0.0 copy-done
  9.1 0.4 %shard_map.65 = bf16[8,7,2,8,128]{4,3,2,1,0:T(8,128)(2,1)S(1)} custom-call(bf16[8,3840]{1,0:T(8,128)(2,1)S(1)} %collective-permute-done.near_ref, bf16[2,8,3840]{2,1,0:T(8,128)(2,1)S(1)} %get-tuple-element.22.far_ref, bf16[112,1152]{1,0:T(8,128)(2,1)S(1)} %get-tuple-element.19.stack_ref, bf16[224,176]{1,0:T(8,128)(2,1)S(1)} %get-tuple-element.20.stencil_ref, ...), custom_call_target="tpu_custom_call" | custom-call | flops 254803968 | bytes 2654208 | tf_op jit(solution)/shard_map/pallas_call | solution.py:362
  9.5 10.9 %all_to_all.15.source_ref = bf16[8,7,2,8,128]{4,3,2,1,0:T(8,128)(2,1)S(1)} all-to-all(bf16[8,7,2,8,128]{4,3,2,1,0:T(8,128)(2,1)S(1)} %shard_map.65), channel_id=1, replica_groups={{3,5,7,6,4,2,0,1},{11,13,15,14,12,10,8,9},{19,21,23,22,20,18,16,17},{27..., dimensions={0} | all-to-all | bytes 458752 | tf_op jit(solution)/shard_map/all_to_all | solution.py:373
  20.3 0.3 shard_map.66
  20.6 8.5 %all_to_all.16.source_ref = bf16[8,7,2,8,128]{4,3,2,1,0:T(8,128)(2,1)S(1)} all-to-all(bf16[8,7,2,8,128]{4,3,2,1,0:T(8,128)(2,1)S(1)} %shard_map.66), channel_id=1, replica_groups={{3,5,7,6,4,2,0,1},{11,13,15,14,12,10,8,9},{19,21,23,22,20,18,16,17},{27..., dimensions={0} | all-to-all | bytes 458752 | tf_op jit(solution)/shard_map/all_to_all | solution.py:373
  29.1 0.7 %shard_map.67 = bf16[6,2,8,1152]{3,2,1,0:T(8,128)(2,1)} custom-call(bf16[8,7,2,8,128]{4,3,2,1,0:T(8,128)(2,1)S(1)} %all_to_all.16.source_ref), custom_call_target="tpu_custom_call" | custom-call | flops 110592 | bytes 442368 | tf_op jit(solution)/shard_map/pallas_call | solution.py:385
  (1 shorter events, 0.0 us)
Async XLA Ops:
  0.0 9.1 %copy-start = (bf16[1152,1152]{1,0:T(8,128)(2,1)S(1)}, bf16[1152,1152]{1,0:T(8,128)(2,1)}, u32[]{:S(2)}) copy-start(bf16[1152,1152]{1,0:T(8,128)(2,1)} %filter_ref.1) | copy-start | bytes 7962628
  1.4 7.6 %collective-permute-start = (bf16[8,3840]{1,0:T(8,128)(2,1)S(1)}, bf16[8,3840]{1,0:T(8,128)(2,1)S(1)}, u32[]{:S(2)}, u32[]{:S(2)}) collective-permute-start(bf16[8,3840]{1,0:T(8,128)(2,1)S(1)} %get-tuple-element.17), channel_id=1, source_target_pairs={{0,8},{16,24},{8,0},{24,16},{1,9},{17,25},{9,1},{25,17},{2,10},{18... | collective-permute-start | bytes 184328 | tf_op jit(solution)/shard_map/ppermute | solution.py:348

commit v2 on v1

--- a/solution.py
+++ b/solution.py
@@ -24,8 +24,8 @@
 
 
 def exchange_order(count):
-    order = list(range(count - 2, -1, -2)) + list(range(1, count, 2))
-    return order[-3:] + order[:-3]
+    order = list(range(count - 1, 0, -2)) + list(range(0, count, 2))
+    return order[1:] + order[:1]
 
 
 def member_at(position, count):

time: 30.3 us -> 29.5 us (0.974)
  blocking collectives: 26.9 us -> 26 us
    all_to_all x2, blocking collectives: 19.4 us -> 18.5 us  [exchange(): lax.all_to_all(array, 'lev', split_axis=0, concat_axis=0, tiled=True, axi...]
where the time goes in v2:
time: 29.5 us; the launch traced here: 29 us
  blocking collectives  26 us (88%)
  Pallas kernels  2.79 us (9%)
    all_to_all x2, blocking collectives, exchange(): lax.all_to_all(array, 'lev', split_axis=0, concat_axis=0, tiled=True, axi...  18.5 us
    all_to_all x1, blocking collectives, exchange_far(): lax.all_to_all(array, 'lat', split_axis=0, concat_axis=0, tiled=True, axi...  7.51 us
    pallas_call x1, Pallas kernels, on_device(): pl.pallas_call(functools.partial(edges_body, **sizes), out_shape=(edges,...  1.43 us
    pallas_call x1, Pallas kernels, on_device(): pl.pallas_call(collect_body, out_shape=array(*fields.shape), in_specs=[WH...  0.74 us
  transfers between devices with their start and end apart: 1, of which 0 were waited for; matrix products, arithmetic and copies ran while one was open for 0% of the time, Pallas kernels for 0%

profile of v2, /device:TPU:1, one launch (start us, length us, event | category | flops | bytes accessed | tf_op | source)
XLA Modules:
  0.0 29.0 jit_solution(16356122427173744989)
XLA Ops:
  0.0 0.0 copy-start
  0.0 1.4 %shard_map.64 = (bf16[8,3840]{1,0:T(8,128)(2,1)S(1)}, bf16[2,8,3840]{2,1,0:T(8,128)(2,1)S(1)}, bf16[112,1152]{1,0:T(8,128)(2,1)S(1)}, bf16[224,176]{1,0:T(8,128)...) custom-call(bf16[1152,1152]{1,0:T(8,128)(2,1)} %filter_ref.1, bf16[96,1152]{1,0:T(8,128)(2,1)} %bitcast.5, ...), custom_call_target="tpu_custom_call" | custom-call | flops 28901376 | bytes 516096 | tf_op jit(solution)/shard_map/pallas_call | solution.py:329
  1.4 0.1 collective-permute-start
  1.6 7.5 %conditional.1 = (bf16[2,8,3840]{2,1,0:T(8,128)(2,1)S(1)}) conditional(s32[]{:T(128)} %convert_element_type.3, bf16[2,8,3840]{2,1,0:T(8,128)(2,1)S(1)} %get-tuple-element.18, bf16[2,8,3840]{2,1,0:T(8,128)(2,1)S(1)} %get-tuple-element.18), branch_computations={%region_0.0_spmd, %region_1.0_spmd} | conditional | bytes 491528 | solution.py:360
  1.6 7.5 %all_to_all.14 = bf16[2,8,3840]{2,1,0:T(8,128)(2,1)S(1)} all-to-all(bf16[2,8,3840]{2,1,0:T(8,128)(2,1)S(1)} %copy.9), channel_id=1, replica_groups={{8,16},{0,24},{9,17},{1,25},{10,18},{2,26},{11,19},{3,27},{12,20},{4,28..., dimensions={0} | all-to-all | bytes 245760 | tf_op jit(solution)/shard_map/cond/branch_1_fun/all_to_all | solution.py:354
  9.1 0.0 collective-permute-done.near_ref
  9.1 0.0 copy-done
  9.1 0.4 %shard_map.65 = bf16[8,7,2,8,128]{4,3,2,1,0:T(8,128)(2,1)S(1)} custom-call(bf16[8,3840]{1,0:T(8,128)(2,1)S(1)} %collective-permute-done.near_ref, bf16[2,8,3840]{2,1,0:T(8,128)(2,1)S(1)} %get-tuple-element.22.far_ref, bf16[112,1152]{1,0:T(8,128)(2,1)S(1)} %get-tuple-element.19.stack_ref, bf16[224,176]{1,0:T(8,128)(2,1)S(1)} %get-tuple-element.20.stencil_ref, ...), custom_call_target="tpu_custom_call" | custom-call | flops 254803968 | bytes 2654208 | tf_op jit(solution)/shard_map/pallas_call | solution.py:362
  9.5 10.0 %all_to_all.15.source_ref = bf16[8,7,2,8,128]{4,3,2,1,0:T(8,128)(2,1)S(1)} all-to-all(bf16[8,7,2,8,128]{4,3,2,1,0:T(8,128)(2,1)S(1)} %shard_map.65), channel_id=1, replica_groups={{5,3,1,0,2,4,6,7},{13,11,9,8,10,12,14,15},{21,19,17,16,18,20,22,23},{29..., dimensions={0} | all-to-all | bytes 458752 | tf_op jit(solution)/shard_map/all_to_all | solution.py:373
  19.5 0.3 shard_map.66
  19.8 8.5 %all_to_all.16.source_ref = bf16[8,7,2,8,128]{4,3,2,1,0:T(8,128)(2,1)S(1)} all-to-all(bf16[8,7,2,8,128]{4,3,2,1,0:T(8,128)(2,1)S(1)} %shard_map.66), channel_id=1, replica_groups={{5,3,1,0,2,4,6,7},{13,11,9,8,10,12,14,15},{21,19,17,16,18,20,22,23},{29..., dimensions={0} | all-to-all | bytes 458752 | tf_op jit(solution)/shard_map/all_to_all | solution.py:373
  28.3 0.7 %shard_map.67 = bf16[6,2,8,1152]{3,2,1,0:T(8,128)(2,1)} custom-call(bf16[8,7,2,8,128]{4,3,2,1,0:T(8,128)(2,1)S(1)} %all_to_all.16.source_ref), custom_call_target="tpu_custom_call" | custom-call | flops 110592 | bytes 442368 | tf_op jit(solution)/shard_map/pallas_call | solution.py:385
  (1 shorter events, 0.0 us)
Async XLA Ops:
  0.0 9.1 %copy-start = (bf16[1152,1152]{1,0:T(8,128)(2,1)S(1)}, bf16[1152,1152]{1,0:T(8,128)(2,1)}, u32[]{:S(2)}) copy-start(bf16[1152,1152]{1,0:T(8,128)(2,1)} %filter_ref.1) | copy-start | bytes 7962628
  1.4 7.6 %collective-permute-start = (bf16[8,3840]{1,0:T(8,128)(2,1)S(1)}, bf16[8,3840]{1,0:T(8,128)(2,1)S(1)}, u32[]{:S(2)}, u32[]{:S(2)}) collective-permute-start(bf16[8,3840]{1,0:T(8,128)(2,1)S(1)} %get-tuple-element.17), channel_id=1, source_target_pairs={{0,8},{16,24},{8,0},{24,16},{1,9},{17,25},{9,1},{25,17},{2,10},{18... | collective-permute-start | bytes 184328 | tf_op jit(solution)/shard_map/ppermute | solution.py:348

commit v3 on v2

--- a/solution.py
+++ b/solution.py
@@ -24,8 +24,8 @@
 
 
 def exchange_order(count):
-    order = list(range(count - 1, 0, -2)) + list(range(0, count, 2))
-    return order[1:] + order[:1]
+    order = list(range(count))[::-1]
+    return order[2:] + order[:2]
 
 
 def member_at(position, count):
@@ -170,11 +170,11 @@
     blocks = own // rows
     field_rows = field_count * levels * rows
     pairs = (
-        (fields_hbm, stack_ref.at[pl.ds(0, field_rows)]),
-        (courant_hbm, stack_ref.at[pl.ds(field_rows, own - field_rows)]),
         (weight_hbm, weight_ref),
         (band_hbm, band_ref),
         (mask_hbm, mask_ref),
+        (fields_hbm, stack_ref.at[pl.ds(0, field_rows)]),
+        (courant_hbm, stack_ref.at[pl.ds(field_rows, own - field_rows)]),
     )
     copies = [
         pltpu.make_async_copy(source, target, sems.at[index])
@@ -194,10 +194,10 @@
     wanted = jnp.where(block < blocks, block * rows + row, -1)
     pick = jnp.where(iota((2 * EDGE_ROWS, own), 1) == wanted, 1.0, 0.0).astype(jnp.bfloat16)
     write_stencil(stencil_ref, field_count, levels, rows)
-    for copy in copies[2:]:
+    for copy in copies[:3]:
         copy.wait()
     write_band_matrix(band_matrix_ref, polar_ref, mask_ref, band_ref, weight_ref, rows, levels)
-    for copy in copies[:2]:
+    for copy in copies[3:]:
         copy.wait()
     edges = jnp.dot(pick, stack_ref[...], preferred_element_type=jnp.float32)
     write_edges(near_ref, edges[:EDGE_ROWS], field_edges, levels)

time: 29.5 us -> 28.8 us (0.976); the launches traced: 29 us -> 28.6 us
  no operation moved by 1% of the time
where the time goes in v3:
time: 28.8 us; the launch traced here: 28.6 us
  blocking collectives  25.8 us (90%)
  Pallas kernels  2.72 us (9%)
    all_to_all x2, blocking collectives, exchange(): lax.all_to_all(array, 'lev', split_axis=0, concat_axis=0, tiled=True, axi...  18.2 us
    all_to_all x1, blocking collectives, exchange_far(): lax.all_to_all(array, 'lat', split_axis=0, concat_axis=0, tiled=True, axi...  7.51 us
    pallas_call x1, Pallas kernels, on_device(): pl.pallas_call(functools.partial(edges_body, **sizes), out_shape=(edges,...  1.36 us
    pallas_call x1, Pallas kernels, on_device(): pl.pallas_call(collect_body, out_shape=array(*fields.shape), in_specs=[WH...  0.74 us
  transfers between devices with their start and end apart: 1, of which 0 were waited for; matrix products, arithmetic and copies ran while one was open for 0% of the time, Pallas kernels for 0%

profile of v3, /device:TPU:1, one launch (start us, length us, event | category | flops | bytes accessed | tf_op | source)
XLA Modules:
  0.0 28.6 jit_solution(15162035206054911960)
XLA Ops:
  0.0 0.0 copy-start
  0.0 1.4 %shard_map.64 = (bf16[8,3840]{1,0:T(8,128)(2,1)S(1)}, bf16[2,8,3840]{2,1,0:T(8,128)(2,1)S(1)}, bf16[112,1152]{1,0:T(8,128)(2,1)S(1)}, bf16[224,176]{1,0:T(8,128)...) custom-call(bf16[1152,1152]{1,0:T(8,128)(2,1)} %filter_ref.1, bf16[96,1152]{1,0:T(8,128)(2,1)} %bitcast.5, ...), custom_call_target="tpu_custom_call" | custom-call | flops 28901376 | bytes 516096 | tf_op jit(solution)/shard_map/pallas_call | solution.py:329
  1.4 0.1 collective-permute-start
  1.5 7.5 %conditional.1 = (bf16[2,8,3840]{2,1,0:T(8,128)(2,1)S(1)}) conditional(s32[]{:T(128)} %convert_element_type.3, bf16[2,8,3840]{2,1,0:T(8,128)(2,1)S(1)} %get-tuple-element.18, bf16[2,8,3840]{2,1,0:T(8,128)(2,1)S(1)} %get-tuple-element.18), branch_computations={%region_0.0_spmd, %region_1.0_spmd} | conditional | bytes 491528 | solution.py:360
  1.5 7.5 %all_to_all.14 = bf16[2,8,3840]{2,1,0:T(8,128)(2,1)S(1)} all-to-all(bf16[2,8,3840]{2,1,0:T(8,128)(2,1)S(1)} %copy.9), channel_id=1, replica_groups={{8,16},{0,24},{9,17},{1,25},{10,18},{2,26},{11,19},{3,27},{12,20},{4,28..., dimensions={0} | all-to-all | bytes 245760 | tf_op jit(solution)/shard_map/cond/branch_1_fun/all_to_all | solution.py:354
  9.0 0.0 collective-permute-done.near_ref
  9.0 0.0 copy-done
  9.0 0.4 %shard_map.65 = bf16[8,7,2,8,128]{4,3,2,1,0:T(8,128)(2,1)S(1)} custom-call(bf16[8,3840]{1,0:T(8,128)(2,1)S(1)} %collective-permute-done.near_ref, bf16[2,8,3840]{2,1,0:T(8,128)(2,1)S(1)} %get-tuple-element.22.far_ref, bf16[112,1152]{1,0:T(8,128)(2,1)S(1)} %get-tuple-element.19.stack_ref, bf16[224,176]{1,0:T(8,128)(2,1)S(1)} %get-tuple-element.20.stencil_ref, ...), custom_call_target="tpu_custom_call" | custom-call | flops 254803968 | bytes 2654208 | tf_op jit(solution)/shard_map/pallas_call | solution.py:362
  9.4 9.1 %all_to_all.15.source_ref = bf16[8,7,2,8,128]{4,3,2,1,0:T(8,128)(2,1)S(1)} all-to-all(bf16[8,7,2,8,128]{4,3,2,1,0:T(8,128)(2,1)S(1)} %shard_map.65), channel_id=1, replica_groups={{5,4,3,2,1,0,7,6},{13,12,11,10,9,8,15,14},{21,20,19,18,17,16,23,22},{29..., dimensions={0} | all-to-all | bytes 458752 | tf_op jit(solution)/shard_map/all_to_all | solution.py:373
  18.5 0.3 shard_map.66
  18.8 9.1 %all_to_all.16.source_ref = bf16[8,7,2,8,128]{4,3,2,1,0:T(8,128)(2,1)S(1)} all-to-all(bf16[8,7,2,8,128]{4,3,2,1,0:T(8,128)(2,1)S(1)} %shard_map.66), channel_id=1, replica_groups={{5,4,3,2,1,0,7,6},{13,12,11,10,9,8,15,14},{21,20,19,18,17,16,23,22},{29..., dimensions={0} | all-to-all | bytes 458752 | tf_op jit(solution)/shard_map/all_to_all | solution.py:373
  27.9 0.7 %shard_map.67 = bf16[6,2,8,1152]{3,2,1,0:T(8,128)(2,1)} custom-call(bf16[8,7,2,8,128]{4,3,2,1,0:T(8,128)(2,1)S(1)} %all_to_all.16.source_ref), custom_call_target="tpu_custom_call" | custom-call | flops 110592 | bytes 442368 | tf_op jit(solution)/shard_map/pallas_call | solution.py:385
  (1 shorter events, 0.0 us)
Async XLA Ops:
  0.0 9.0 %copy-start = (bf16[1152,1152]{1,0:T(8,128)(2,1)S(1)}, bf16[1152,1152]{1,0:T(8,128)(2,1)}, u32[]{:S(2)}) copy-start(bf16[1152,1152]{1,0:T(8,128)(2,1)} %filter_ref.1) | copy-start | bytes 7962628
  1.4 7.6 %collective-permute-start = (bf16[8,3840]{1,0:T(8,128)(2,1)S(1)}, bf16[8,3840]{1,0:T(8,128)(2,1)S(1)}, u32[]{:S(2)}, u32[]{:S(2)}) collective-permute-start(bf16[8,3840]{1,0:T(8,128)(2,1)S(1)} %get-tuple-element.17), channel_id=1, source_target_pairs={{0,8},{16,24},{8,0},{24,16},{1,9},{17,25},{9,1},{25,17},{2,10},{18... | collective-permute-start | bytes 184328 | tf_op jit(solution)/shard_map/ppermute | solution.py:348

commit v4 on v3

--- a/solution.py
+++ b/solution.py
@@ -25,7 +25,7 @@
 
 def exchange_order(count):
     order = list(range(count))[::-1]
-    return order[2:] + order[:2]
+    return order[3:] + order[:3]
 
 
 def member_at(position, count):

time: 28.8 us -> 29 us (level)
  no operation moved by 1% of the time
where the time goes in v4:
time: 29 us; the launch traced here: 28.8 us
  blocking collectives  25.9 us (89%)
  Pallas kernels  2.72 us (9%)
    all_to_all x2, blocking collectives, exchange(): lax.all_to_all(array, 'lev', split_axis=0, concat_axis=0, tiled=True, axi...  18.4 us
    all_to_all x1, blocking collectives, exchange_far(): lax.all_to_all(array, 'lat', split_axis=0, concat_axis=0, tiled=True, axi...  7.51 us
    pallas_call x1, Pallas kernels, on_device(): pl.pallas_call(functools.partial(edges_body, **sizes), out_shape=(edges,...  1.36 us
    pallas_call x1, Pallas kernels, on_device(): pl.pallas_call(collect_body, out_shape=array(*fields.shape), in_specs=[WH...  0.74 us
  transfers between devices with their start and end apart: 1, of which 0 were waited for; matrix products, arithmetic and copies ran while one was open for 0% of the time, Pallas kernels for 0%

profile of v4, /device:TPU:1, one launch (start us, length us, event | category | flops | bytes accessed | tf_op | source)
XLA Modules:
  0.0 28.8 jit_solution(10897790237859664135)
XLA Ops:
  0.0 0.0 copy-start
  0.0 1.4 %shard_map.64 = (bf16[8,3840]{1,0:T(8,128)(2,1)S(1)}, bf16[2,8,3840]{2,1,0:T(8,128)(2,1)S(1)}, bf16[112,1152]{1,0:T(8,128)(2,1)S(1)}, bf16[224,176]{1,0:T(8,128)...) custom-call(bf16[1152,1152]{1,0:T(8,128)(2,1)} %filter_ref.1, bf16[96,1152]{1,0:T(8,128)(2,1)} %bitcast.5, ...), custom_call_target="tpu_custom_call" | custom-call | flops 28901376 | bytes 516096 | tf_op jit(solution)/shard_map/pallas_call | solution.py:329
  1.4 0.1 collective-permute-start
  1.5 7.5 %conditional.1 = (bf16[2,8,3840]{2,1,0:T(8,128)(2,1)S(1)}) conditional(s32[]{:T(128)} %convert_element_type.3, bf16[2,8,3840]{2,1,0:T(8,128)(2,1)S(1)} %get-tuple-element.18, bf16[2,8,3840]{2,1,0:T(8,128)(2,1)S(1)} %get-tuple-element.18), branch_computations={%region_0.0_spmd, %region_1.0_spmd} | conditional | bytes 491528 | solution.py:360
  1.5 7.5 %all_to_all.14 = bf16[2,8,3840]{2,1,0:T(8,128)(2,1)S(1)} all-to-all(bf16[2,8,3840]{2,1,0:T(8,128)(2,1)S(1)} %copy.9), channel_id=1, replica_groups={{8,16},{0,24},{9,17},{1,25},{10,18},{2,26},{11,19},{3,27},{12,20},{4,28..., dimensions={0} | all-to-all | bytes 245760 | tf_op jit(solution)/shard_map/cond/branch_1_fun/all_to_all | solution.py:354
  9.0 0.0 collective-permute-done.near_ref
  9.0 0.0 copy-done
  9.0 0.4 %shard_map.65 = bf16[8,7,2,8,128]{4,3,2,1,0:T(8,128)(2,1)S(1)} custom-call(bf16[8,3840]{1,0:T(8,128)(2,1)S(1)} %collective-permute-done.near_ref, bf16[2,8,3840]{2,1,0:T(8,128)(2,1)S(1)} %get-tuple-element.22.far_ref, bf16[112,1152]{1,0:T(8,128)(2,1)S(1)} %get-tuple-element.19.stack_ref, bf16[224,176]{1,0:T(8,128)(2,1)S(1)} %get-tuple-element.20.stencil_ref, ...), custom_call_target="tpu_custom_call" | custom-call | flops 254803968 | bytes 2654208 | tf_op jit(solution)/shard_map/pallas_call | solution.py:362
  9.4 9.4 %all_to_all.15.source_ref = bf16[8,7,2,8,128]{4,3,2,1,0:T(8,128)(2,1)S(1)} all-to-all(bf16[8,7,2,8,128]{4,3,2,1,0:T(8,128)(2,1)S(1)} %shard_map.65), channel_id=1, replica_groups={{4,3,2,1,0,7,6,5},{12,11,10,9,8,15,14,13},{20,19,18,17,16,23,22,21},{28..., dimensions={0} | all-to-all | bytes 458752 | tf_op jit(solution)/shard_map/all_to_all | solution.py:373
  18.8 0.3 shard_map.66
  19.1 8.9 %all_to_all.16.source_ref = bf16[8,7,2,8,128]{4,3,2,1,0:T(8,128)(2,1)S(1)} all-to-all(bf16[8,7,2,8,128]{4,3,2,1,0:T(8,128)(2,1)S(1)} %shard_map.66), channel_id=1, replica_groups={{4,3,2,1,0,7,6,5},{12,11,10,9,8,15,14,13},{20,19,18,17,16,23,22,21},{28..., dimensions={0} | all-to-all | bytes 458752 | tf_op jit(solution)/shard_map/all_to_all | solution.py:373
  28.0 0.7 %shard_map.67 = bf16[6,2,8,1152]{3,2,1,0:T(8,128)(2,1)} custom-call(bf16[8,7,2,8,128]{4,3,2,1,0:T(8,128)(2,1)S(1)} %all_to_all.16.source_ref), custom_call_target="tpu_custom_call" | custom-call | flops 110592 | bytes 442368 | tf_op jit(solution)/shard_map/pallas_call | solution.py:385
  (1 shorter events, 0.0 us)
Async XLA Ops:
  0.0 9.0 %copy-start = (bf16[1152,1152]{1,0:T(8,128)(2,1)S(1)}, bf16[1152,1152]{1,0:T(8,128)(2,1)}, u32[]{:S(2)}) copy-start(bf16[1152,1152]{1,0:T(8,128)(2,1)} %filter_ref.1) | copy-start | bytes 7962628
  1.4 7.6 %collective-permute-start = (bf16[8,3840]{1,0:T(8,128)(2,1)S(1)}, bf16[8,3840]{1,0:T(8,128)(2,1)S(1)}, u32[]{:S(2)}, u32[]{:S(2)}) collective-permute-start(bf16[8,3840]{1,0:T(8,128)(2,1)S(1)} %get-tuple-element.17), channel_id=1, source_target_pairs={{0,8},{16,24},{8,0},{24,16},{1,9},{17,25},{9,1},{25,17},{2,10},{18... | collective-permute-start | bytes 184328 | tf_op jit(solution)/shard_map/ppermute | solution.py:348

commit v5 on v3

--- a/solution.py
+++ b/solution.py
@@ -24,7 +24,7 @@
 
 
 def exchange_order(count):
-    order = list(range(count))[::-1]
+    order = [index ^ (index // 2 % 2 == 1) for index in range(count)][::-1]
     return order[2:] + order[:2]
 
 

time: 28.8 us -> 29 us (level)
  no operation moved by 1% of the time
where the time goes in v5:
time: 29 us; the launch traced here: 28.8 us
  blocking collectives  25.9 us (89%)
  Pallas kernels  2.72 us (9%)
    all_to_all x2, blocking collectives, exchange(): lax.all_to_all(array, 'lev', split_axis=0, concat_axis=0, tiled=True, axi...  18.4 us
    all_to_all x1, blocking collectives, exchange_far(): lax.all_to_all(array, 'lat', split_axis=0, concat_axis=0, tiled=True, axi...  7.51 us
    pallas_call x1, Pallas kernels, on_device(): pl.pallas_call(functools.partial(edges_body, **sizes), out_shape=(edges,...  1.36 us
    pallas_call x1, Pallas kernels, on_device(): pl.pallas_call(collect_body, out_shape=array(*fields.shape), in_specs=[WH...  0.74 us
  transfers between devices with their start and end apart: 1, of which 0 were waited for; matrix products, arithmetic and copies ran while one was open for 0% of the time, Pallas kernels for 0%

profile of v5, /device:TPU:1, one launch (start us, length us, event | category | flops | bytes accessed | tf_op | source)
XLA Modules:
  0.0 28.8 jit_solution(8146435715071170035)
XLA Ops:
  0.0 0.0 copy-start
  0.0 1.4 %shard_map.64 = (bf16[8,3840]{1,0:T(8,128)(2,1)S(1)}, bf16[2,8,3840]{2,1,0:T(8,128)(2,1)S(1)}, bf16[112,1152]{1,0:T(8,128)(2,1)S(1)}, bf16[224,176]{1,0:T(8,128)...) custom-call(bf16[1152,1152]{1,0:T(8,128)(2,1)} %filter_ref.1, bf16[96,1152]{1,0:T(8,128)(2,1)} %bitcast.5, ...), custom_call_target="tpu_custom_call" | custom-call | flops 28901376 | bytes 516096 | tf_op jit(solution)/shard_map/pallas_call | solution.py:329
  1.4 0.1 collective-permute-start
  1.5 7.5 %conditional.1 = (bf16[2,8,3840]{2,1,0:T(8,128)(2,1)S(1)}) conditional(s32[]{:T(128)} %convert_element_type.3, bf16[2,8,3840]{2,1,0:T(8,128)(2,1)S(1)} %get-tuple-element.18, bf16[2,8,3840]{2,1,0:T(8,128)(2,1)S(1)} %get-tuple-element.18), branch_computations={%region_0.0_spmd, %region_1.0_spmd} | conditional | bytes 491528 | solution.py:360
  1.5 7.5 %all_to_all.14 = bf16[2,8,3840]{2,1,0:T(8,128)(2,1)S(1)} all-to-all(bf16[2,8,3840]{2,1,0:T(8,128)(2,1)S(1)} %copy.9), channel_id=1, replica_groups={{8,16},{0,24},{9,17},{1,25},{10,18},{2,26},{11,19},{3,27},{12,20},{4,28..., dimensions={0} | all-to-all | bytes 245760 | tf_op jit(solution)/shard_map/cond/branch_1_fun/all_to_all | solution.py:354
  9.0 0.0 collective-permute-done.near_ref
  9.0 0.0 copy-done
  9.0 0.4 %shard_map.65 = bf16[8,7,2,8,128]{4,3,2,1,0:T(8,128)(2,1)S(1)} custom-call(bf16[8,3840]{1,0:T(8,128)(2,1)S(1)} %collective-permute-done.near_ref, bf16[2,8,3840]{2,1,0:T(8,128)(2,1)S(1)} %get-tuple-element.22.far_ref, bf16[112,1152]{1,0:T(8,128)(2,1)S(1)} %get-tuple-element.19.stack_ref, bf16[224,176]{1,0:T(8,128)(2,1)S(1)} %get-tuple-element.20.stencil_ref, ...), custom_call_target="tpu_custom_call" | custom-call | flops 254803968 | bytes 2654208 | tf_op jit(solution)/shard_map/pallas_call | solution.py:362
  9.4 9.1 %all_to_all.15.source_ref = bf16[8,7,2,8,128]{4,3,2,1,0:T(8,128)(2,1)S(1)} all-to-all(bf16[8,7,2,8,128]{4,3,2,1,0:T(8,128)(2,1)S(1)} %shard_map.65), channel_id=1, replica_groups={{5,4,2,3,1,0,6,7},{13,12,10,11,9,8,14,15},{21,20,18,19,17,16,22,23},{29..., dimensions={0} | all-to-all | bytes 458752 | tf_op jit(solution)/shard_map/all_to_all | solution.py:373
  18.5 0.3 shard_map.66
  18.8 9.3 %all_to_all.16.source_ref = bf16[8,7,2,8,128]{4,3,2,1,0:T(8,128)(2,1)S(1)} all-to-all(bf16[8,7,2,8,128]{4,3,2,1,0:T(8,128)(2,1)S(1)} %shard_map.66), channel_id=1, replica_groups={{5,4,2,3,1,0,6,7},{13,12,10,11,9,8,14,15},{21,20,18,19,17,16,22,23},{29..., dimensions={0} | all-to-all | bytes 458752 | tf_op jit(solution)/shard_map/all_to_all | solution.py:373
  28.1 0.7 %shard_map.67 = bf16[6,2,8,1152]{3,2,1,0:T(8,128)(2,1)} custom-call(bf16[8,7,2,8,128]{4,3,2,1,0:T(8,128)(2,1)S(1)} %all_to_all.16.source_ref), custom_call_target="tpu_custom_call" | custom-call | flops 110592 | bytes 442368 | tf_op jit(solution)/shard_map/pallas_call | solution.py:385
  (1 shorter events, 0.0 us)
Async XLA Ops:
  0.0 9.0 %copy-start = (bf16[1152,1152]{1,0:T(8,128)(2,1)S(1)}, bf16[1152,1152]{1,0:T(8,128)(2,1)}, u32[]{:S(2)}) copy-start(bf16[1152,1152]{1,0:T(8,128)(2,1)} %filter_ref.1) | copy-start | bytes 7962628
  1.4 7.6 %collective-permute-start = (bf16[8,3840]{1,0:T(8,128)(2,1)S(1)}, bf16[8,3840]{1,0:T(8,128)(2,1)S(1)}, u32[]{:S(2)}, u32[]{:S(2)}) collective-permute-start(bf16[8,3840]{1,0:T(8,128)(2,1)S(1)} %get-tuple-element.17), channel_id=1, source_target_pairs={{0,8},{16,24},{8,0},{24,16},{1,9},{17,25},{9,1},{25,17},{2,10},{18... | collective-permute-start | bytes 184328 | tf_op jit(solution)/shard_map/ppermute | solution.py:348

commit v6 on v5

--- a/solution.py
+++ b/solution.py
@@ -24,8 +24,9 @@
 
 
 def exchange_order(count):
-    order = [index ^ (index // 2 % 2 == 1) for index in range(count)][::-1]
-    return order[2:] + order[:2]
+    order = [index ^ 1 for index in range(count)][::-1]
+    order = order[2:] + order[:2]
+    return order[1::-1] + order[2:]
 
 
 def member_at(position, count):

time: 29 us -> 28.7 us (0.990)
  blocking collectives: 25.9 us -> 25.6 us
where the time goes in v6:
time: 28.7 us; the launch traced here: 28.5 us
  blocking collectives  25.6 us (89%)
  Pallas kernels  2.72 us (9%)
    all_to_all x2, blocking collectives, exchange(): lax.all_to_all(array, 'lev', split_axis=0, concat_axis=0, tiled=True, axi...  18.1 us
    all_to_all x1, blocking collectives, exchange_far(): lax.all_to_all(array, 'lat', split_axis=0, concat_axis=0, tiled=True, axi...  7.51 us
    pallas_call x1, Pallas kernels, on_device(): pl.pallas_call(functools.partial(edges_body, **sizes), out_shape=(edges,...  1.36 us
    pallas_call x1, Pallas kernels, on_device(): pl.pallas_call(collect_body, out_shape=array(*fields.shape), in_specs=[WH...  0.74 us
  transfers between devices with their start and end apart: 1, of which 0 were waited for; matrix products, arithmetic and copies ran while one was open for 0% of the time, Pallas kernels for 0%

profile of v6, /device:TPU:1, one launch (start us, length us, event | category | flops | bytes accessed | tf_op | source)
XLA Modules:
  0.0 28.5 jit_solution(8904121168865155448)
XLA Ops:
  0.0 0.0 copy-start
  0.0 1.4 %shard_map.64 = (bf16[8,3840]{1,0:T(8,128)(2,1)S(1)}, bf16[2,8,3840]{2,1,0:T(8,128)(2,1)S(1)}, bf16[112,1152]{1,0:T(8,128)(2,1)S(1)}, bf16[224,176]{1,0:T(8,128)...) custom-call(bf16[1152,1152]{1,0:T(8,128)(2,1)} %filter_ref.1, bf16[96,1152]{1,0:T(8,128)(2,1)} %bitcast.5, ...), custom_call_target="tpu_custom_call" | custom-call | flops 28901376 | bytes 516096 | tf_op jit(solution)/shard_map/pallas_call | solution.py:330
  1.4 0.1 collective-permute-start
  1.5 7.5 %conditional.1 = (bf16[2,8,3840]{2,1,0:T(8,128)(2,1)S(1)}) conditional(s32[]{:T(128)} %convert_element_type.3, bf16[2,8,3840]{2,1,0:T(8,128)(2,1)S(1)} %get-tuple-element.18, bf16[2,8,3840]{2,1,0:T(8,128)(2,1)S(1)} %get-tuple-element.18), branch_computations={%region_0.0_spmd, %region_1.0_spmd} | conditional | bytes 491528 | solution.py:361
  1.5 7.5 %all_to_all.14 = bf16[2,8,3840]{2,1,0:T(8,128)(2,1)S(1)} all-to-all(bf16[2,8,3840]{2,1,0:T(8,128)(2,1)S(1)} %copy.9), channel_id=1, replica_groups={{8,16},{0,24},{9,17},{1,25},{10,18},{2,26},{11,19},{3,27},{12,20},{4,28..., dimensions={0} | all-to-all | bytes 245760 | tf_op jit(solution)/shard_map/cond/branch_1_fun/all_to_all | solution.py:355
  9.0 0.0 collective-permute-done.near_ref
  9.0 0.0 copy-done
  9.0 0.4 %shard_map.65 = bf16[8,7,2,8,128]{4,3,2,1,0:T(8,128)(2,1)S(1)} custom-call(bf16[8,3840]{1,0:T(8,128)(2,1)S(1)} %collective-permute-done.near_ref, bf16[2,8,3840]{2,1,0:T(8,128)(2,1)S(1)} %get-tuple-element.22.far_ref, bf16[112,1152]{1,0:T(8,128)(2,1)S(1)} %get-tuple-element.19.stack_ref, bf16[224,176]{1,0:T(8,128)(2,1)S(1)} %get-tuple-element.20.stencil_ref, ...), custom_call_target="tpu_custom_call" | custom-call | flops 254803968 | bytes 2654208 | tf_op jit(solution)/shard_map/pallas_call | solution.py:363
  9.4 9.4 %all_to_all.15.source_ref = bf16[8,7,2,8,128]{4,3,2,1,0:T(8,128)(2,1)S(1)} all-to-all(bf16[8,7,2,8,128]{4,3,2,1,0:T(8,128)(2,1)S(1)} %shard_map.65), channel_id=1, replica_groups={{5,4,2,3,0,1,6,7},{13,12,10,11,8,9,14,15},{21,20,18,19,16,17,22,23},{29..., dimensions={0} | all-to-all | bytes 458752 | tf_op jit(solution)/shard_map/all_to_all | solution.py:374
  18.8 0.3 shard_map.66
  19.1 8.7 %all_to_all.16.source_ref = bf16[8,7,2,8,128]{4,3,2,1,0:T(8,128)(2,1)S(1)} all-to-all(bf16[8,7,2,8,128]{4,3,2,1,0:T(8,128)(2,1)S(1)} %shard_map.66), channel_id=1, replica_groups={{5,4,2,3,0,1,6,7},{13,12,10,11,8,9,14,15},{21,20,18,19,16,17,22,23},{29..., dimensions={0} | all-to-all | bytes 458752 | tf_op jit(solution)/shard_map/all_to_all | solution.py:374
  27.8 0.7 %shard_map.67 = bf16[6,2,8,1152]{3,2,1,0:T(8,128)(2,1)} custom-call(bf16[8,7,2,8,128]{4,3,2,1,0:T(8,128)(2,1)S(1)} %all_to_all.16.source_ref), custom_call_target="tpu_custom_call" | custom-call | flops 110592 | bytes 442368 | tf_op jit(solution)/shard_map/pallas_call | solution.py:386
  (1 shorter events, 0.0 us)
Async XLA Ops:
  0.0 9.0 %copy-start = (bf16[1152,1152]{1,0:T(8,128)(2,1)S(1)}, bf16[1152,1152]{1,0:T(8,128)(2,1)}, u32[]{:S(2)}) copy-start(bf16[1152,1152]{1,0:T(8,128)(2,1)} %filter_ref.1) | copy-start | bytes 7962628
  1.4 7.6 %collective-permute-start = (bf16[8,3840]{1,0:T(8,128)(2,1)S(1)}, bf16[8,3840]{1,0:T(8,128)(2,1)S(1)}, u32[]{:S(2)}, u32[]{:S(2)}) collective-permute-start(bf16[8,3840]{1,0:T(8,128)(2,1)S(1)} %get-tuple-element.17), channel_id=1, source_target_pairs={{0,8},{16,24},{8,0},{24,16},{1,9},{17,25},{9,1},{25,17},{2,10},{18... | collective-permute-start | bytes 184328 | tf_op jit(solution)/shard_map/ppermute | solution.py:349
